TPU v7x, 128 devices: a whole 4x4x4 slice. The times are simulated.
128 devices in a mesh: grp: 16 (over x, z), sub: 8 (over y, core).
Axes of the slice: x: 4, y: 4, z: 4, core: 2. Of those that a mesh axis runs over, the one named last changes fastest.
Arguments:
- embed: float32 [98304, 1024], P(('grp', 'sub'))
- cluster: int32 [98304], P(('grp', 'sub')), may hold values from 0 to 1023, as said below
- rank: int32 [98304], P(('grp', 'sub')), may hold values from 0 to 767, as said below
- target: int32 [98304], P(('grp', 'sub')), may hold values from 0 to 98303, as said below
Outputs:
- best: float32 [98304], P(('grp', 'sub'))
Inputs may be any that keep to these rules, and one draw needn't show every extreme that they name: `target`: A permutation: document i goes to row target_i mod 768 of device target_i divided by 768, rounded down, the devices numbered over grp+sub. All documents of one cluster go to devices of one grp index. One device's shard sends at most 12 documents to any one device, and exactly 12 to some. Within a grp index, the row of a document in the group's order (its device's sub index times 768 plus its row) is the number of the group's documents in lower-numbered clusters plus its rank. `cluster`: clusters of one grp index are numbered from that index times 64. `rank`: the ranks inside one cluster are distinct and run from 0 to its size minus 1; the largest cluster of each grp index has 768 documents.
All inputs are finite; a program needn't handle non-finite values.
Results may differ from a plain program's by a relative error of at most 0.00037.
Values may be sent and summed in bfloat16 or wider, within the bound.
A program may use at most 64 MiB of HBM per device.

v0:
```python
import functools

import jax
import jax.numpy as jnp
from jax import lax
from jax.experimental import pallas as pl
from jax.experimental.pallas import tpu as pltpu
from jax.sharding import PartitionSpec as P

MESH = pl.DeviceIdType.MESH
AXES = ("x", "z", "y", "c")
SIZE = {"x": 4, "z": 4, "y": 4, "c": 2}
ORDERS = (("x", "y", "z"), ("y", "z", "x"), ("z", "x", "y"))
ROWS = 768
WIDTH = 1024
HALF = 512
CAP = 12
GROUPS = 3
DEPTH = 4
DEVICES = 128
EDGE = 336
REST = ROWS - EDGE
PARTS = ((0, 256), (256, EDGE), (EDGE, EDGE + 256), (EDGE + 256, ROWS))
NT = (((1,), (1,)), ((), ()))
bf16, f32, i32 = jnp.bfloat16, jnp.float32, jnp.int32


def view(ref, *lead, **fixed):
    return ref.at[tuple(lead) + tuple(fixed.get(a, slice(None)) for a in AXES)]


def iota(shape, dim):
    return lax.broadcasted_iota(i32, shape, dim)


def dot(a, b, dims=(((1,), (0,)), ((), ())), exact=False):
    precision = lax.Precision.HIGHEST if exact else None
    return lax.dot_general(a, b, dims, precision=precision, preferred_element_type=f32)


def kernel(
    embed_hbm, target_hbm, rank_hbm, best_ref,
    target_ref, rank_ref, embed, scale, picks, unit, sent0, sent1, sent2, sent3, meta0, meta1, meta2, meta3, flat,
    slots, chosen, partly, own, from_prev, from_next, with_prev, with_next, returned, answer,
    load_sem, index_sem, sem1, sem2, sem3, out_sem, msem1, msem2, msem3, mout_sem,
    halo_sem, halo_out, last_sem, last_out, back_sem, back_out,
):
    grp, sub = lax.axis_index("grp"), lax.axis_index("sub")
    me = {"x": grp // 4, "z": lax.rem(grp, 4), "y": sub // 2, "c": lax.rem(sub, 2)}

    def device(**other):
        at = {**me, **other}
        return (at["x"] * 4 + at["z"], at["y"] * 2 + at["c"])

    def around(axis, by):
        return lax.rem(me[axis] + by, 4)

    def remote(src, dst, send_sem, recv_sem, to):
        pltpu.make_async_remote_copy(
            src_ref=src, dst_ref=dst, send_sem=send_sem, recv_sem=recv_sem,
            device_id=to, device_id_type=MESH,
        ).start()

    def landed(ref, sem):
        pltpu.make_async_copy(ref, ref, sem).wait()

    indices = [
        pltpu.make_async_copy(target_hbm, target_ref, index_sem.at[0]),
        pltpu.make_async_copy(rank_hbm, rank_ref, index_sem.at[1]),
    ]
    for load in indices:
        load.start()
    loads = []
    for i in range(3):
        part = pl.ds(i * 256, 256)
        loads.append(pltpu.make_async_copy(embed_hbm.at[part], embed.at[part], load_sem.at[i]))
        loads[-1].start()

    barrier = pltpu.get_barrier_semaphore()
    partners = [device(**{a: around(a, d)}) for a in "xyz" for d in (1, 2, 3)]
    partners += [device(**{a: around(a, d), "c": 1 - me["c"]}) for a in "xyz" for d in (1, 2, 3)]
    partners += [device(c=1 - me["c"])]
    for to in partners:
        pl.semaphore_signal(barrier, inc=1, device_id=to, device_id_type=MESH)

    chosen[:, 0:ROWS] = (iota((ROWS, ROWS), 0) < iota((ROWS, ROWS), 1)).astype(f32).astype(bf16)

    for load in indices:
        load.wait()
    target = target_ref[...].reshape(1, ROWS).astype(f32)
    rank = rank_ref[...].reshape(1, ROWS).astype(f32)
    owner = jnp.floor((target + 0.5) * (1.0 / ROWS))
    row = target - owner * ROWS
    owns = (owner == iota((DEVICES, ROWS), 0).astype(f32)).astype(f32)
    count = dot(owns.astype(bf16), chosen[:, 0:ROWS])
    within = jnp.sum(owns * count, axis=0, keepdims=True)
    code = owner * CAP + within
    def pick(g):
        k = iota((DEVICES * DEPTH, ROWS), 0)
        wanted = 3 * k - 2 * (k & 3) + DEPTH * g
        picks[g] = (code.astype(i32) == wanted).astype(f32).astype(bf16)

    pick(1)
    for i in range(3):
        loads[i].wait()

        for j in range(8):
            part = slice(i * 256 + j * 32, i * 256 + j * 32 + 32)
            e = embed[part, :]
            squares = jnp.sum(e * e, axis=1, keepdims=True)
            scale[part, :] = jnp.broadcast_to(lax.rsqrt(squares + 1e-06), (32, 128))
            unit[part, 0:HALF] = (e[:, 0:HALF] * jnp.tile(scale[part, :], (1, 4))).astype(bf16)

    def meta_first():
        lane_slot = iota((DEVICES, ROWS), 0).astype(f32)
        spread = jnp.where(within == lane_slot, row + 1.0, 0.0) + jnp.where(
            within + 16.0 == lane_slot, rank, 0.0
        )
        flat[...] = dot(owns, spread, NT, exact=True)
        for x in range(4):
            for z in range(4):
                for y in range(4):
                    for c in range(2):
                        at = ((x * 4 + z) * 4 + y) * 2 + c
                        meta0[x, z, y, c] = flat[at : at + 1, :]
        for d in (1, 3, 2):
            t = around("x", d)
            remote(view(meta0, x=t), view(meta1, x=me["x"]), mout_sem.at[0], msem1, device(x=t))
        pltpu.make_async_copy(view(meta0, x=me["x"]), view(meta1, x=me["x"]), msem1).start()

    def meta_second():
        landed(meta1, msem1)
        for d in (1, 3, 2):
            t = around("z", d)
            remote(view(meta1, z=t), view(meta2, z=me["z"]), mout_sem.at[1], msem2, device(z=t))
        pltpu.make_async_copy(view(meta1, z=me["z"]), view(meta2, z=me["z"]), msem2).start()

    def meta_third():
        landed(meta2, msem2)
        for d in (1, 3, 2, 0):
            t = around("y", d)
            for c in (me["c"], 1 - me["c"]):
                if d == 0 and c is me["c"]:
                    continue
                remote(
                    view(meta2, y=t, c=c), view(meta3, y=me["y"], c=me["c"]),
                    mout_sem.at[2], msem3, device(y=t, c=c),
                )
        here = {"y": me["y"], "c": me["c"]}
        pltpu.make_async_copy(view(meta2, **here), view(meta3, **here), msem3).start()

    def pack(h, g):
        q = dot(picks[g], unit[:, h * HALF : (h + 1) * HALF]).reshape(64, 8, HALF)
        r = pltpu.roll(q, 4, 1)
        low = iota((64, 8, 128), 1) < 4
        qs = [q[:, :, 128 * j : 128 * j + 128] for j in range(4)]
        rs = [r[:, :, 128 * j : 128 * j + 128] for j in range(4)]
        even = jnp.concatenate([jnp.where(low, qs[0], rs[1]), jnp.where(low, qs[2], rs[3])], axis=1)
        odd = jnp.concatenate([jnp.where(low, rs[0], qs[1]), jnp.where(low, rs[2], qs[3])], axis=1)
        sent0[h, g, :, :, :, 0] = even.astype(bf16).reshape(4, 4, 4, 16, 128)
        sent0[h, g, :, :, :, 1] = odd.astype(bf16).reshape(4, 4, 4, 16, 128)

    def first(h, g):
        a = ORDERS[g][0]
        for d in (1, 3, 2):
            t = around(a, d)
            remote(
                view(sent0, h, g, **{a: t}), view(sent1, h, g, **{a: me[a]}),
                out_sem.at[h, g, 0], sem1.at[h, g, me[a]], device(**{a: t}),
            )
        here = {a: me[a]}
        pltpu.make_async_copy(
            view(sent0, h, g, **here), view(sent1, h, g, **here), sem1.at[h, g, me[a]]
        ).start()

    def second(h, g, d0):
        a, b, _ = ORDERS[g]
        s = around(a, d0)
        landed(view(sent1, h, g, **{a: s}), sem1.at[h, g, s])
        for d in (1, 3, 2):
            t = around(b, d)
            remote(
                view(sent1, h, g, **{a: s, b: t}), view(sent2, h, g, **{a: s, b: me[b]}),
                out_sem.at[h, g, 1], sem2.at[h, g, me[b]], device(**{b: t}),
            )
        here = {a: s, b: me[b]}
        pltpu.make_async_copy(
            view(sent1, h, g, **here), view(sent2, h, g, **here), sem2.at[h, g, me[b]]
        ).start()

    def third(h, g, d0):
        _, b, e = ORDERS[g]
        s = around(b, d0)
        landed(view(sent2, h, g, **{b: s}), sem2.at[h, g, s])
        for d in (1, 3, 2, 0):
            t = around(e, d)
            for c in (me["c"], 1 - me["c"]):
                if d == 0 and c is me["c"]:
                    continue
                remote(
                    view(sent2, h, g, **{b: s, e: t, "c": c}),
                    view(sent3, h, g, **{b: s, e: me[e], "c": me["c"]}),
                    out_sem.at[h, g, 2], sem3.at[h, g], device(**{e: t, "c": c}),
                )
        here = {b: s, e: me[e], "c": me["c"]}
        pltpu.make_async_copy(
            view(sent2, h, g, **here), view(sent3, h, g, **here), sem3.at[h, g]
        ).start()

    def unpack(h, g):
        landed(sent3.at[h, g], sem3.at[h, g])
        even = sent3[h, g, :, :, :, 0].reshape(64, 16, 128).astype(f32)
        odd = sent3[h, g, :, :, :, 1].reshape(64, 16, 128).astype(f32)
        low = iota((64, 8, 128), 1) < 4
        rows = pl.ds(pl.multiple_of(g * 512, 512), 512)
        for j in range(2):
            a, b = even[:, 8 * j : 8 * j + 8], odd[:, 8 * j : 8 * j + 8]
            p = jnp.where(low, a, pltpu.roll(b, 4, 1)).reshape(512, 128)
            q = jnp.where(low, pltpu.roll(a, 4, 1), b).reshape(512, 128)
            slots[h, rows, 256 * j : 256 * j + 128] = p.astype(bf16)
            slots[h, rows, 256 * j + 128 : 256 * j + 256] = q.astype(bf16)

    later = (grp, lax.rem(sub + 1, 8))
    sooner = (grp, lax.rem(sub + 7, 8))

    def halo_sooner(h):
        remote(
            own.at[h, pl.ds(0, EDGE)], from_next.at[h],
            halo_out.at[1], halo_sem.at[1], sooner,
        )

    def halo_later(h):
        remote(
            own.at[h, pl.ds(EDGE, REST)], from_prev.at[h],
            halo_out.at[0], halo_sem.at[0], later,
        )

    def gather():
        own[0, 0:EDGE, :] = dot(chosen[0:EDGE, :], slots[0]).astype(bf16)
        halo_sooner(0)
        own[0, EDGE:ROWS, :] = dot(chosen[EDGE:ROWS, :], slots[0]).astype(bf16)
        halo_later(0)

    def gather_most():
        partly[...] = dot(chosen[:, 0:1024], slots[1, 0:1024])

    def gather_rest():
        for i, (lo, hi) in enumerate(PARTS):
            rest = dot(chosen[lo:hi, 1024:1536], slots[1, 1024:1536])
            own[1, lo:hi, :] = (partly[lo:hi, :] + rest).astype(bf16)
            if hi <= EDGE:
                there, to = from_next.at[1, pl.ds(lo, hi - lo)], sooner
            else:
                there, to = from_prev.at[1, pl.ds(lo - EDGE, hi - lo)], later
            remote(own.at[1, pl.ds(lo, hi - lo)], there, last_out.at[i], last_sem.at[i], to)

    def choose():
        landed(meta3, msem3)
        for x in range(4):
            for z in range(4):
                for y in range(4):
                    for c in range(2):
                        at = ((x * 4 + z) * 4 + y) * 2 + c
                        flat[at : at + 1, :] = meta3[x, z, y, c]
        got = flat[...]
        l, k = iota((128, 768), 0), iota((128, 768), 1)
        g, kind = (k // 128) % 3, k // 384
        expand = (l == kind * 16 + g * DEPTH + (k & 3)).astype(f32)
        wide = dot(got, expand, exact=True)
        mine = (iota((32, 128), 1) >> 2) == iota((32, 128), 0)

        def lanes(first):
            pieces = []
            for g in range(GROUPS):
                for j in range(4):
                    v = wide[32 * j : 32 * j + 32, first + 128 * g : first + 128 * g + 128]
                    pieces.append(jnp.sum(jnp.where(mine, v, 0.0), axis=0, keepdims=True))
            return jnp.concatenate(pieces, axis=1)

        place, its_rank = lanes(0), lanes(384)

        def build(j, _):
            part = pl.ds(pl.multiple_of(j * 64, 64), 64)
            r = (iota((64, 1536), 0) + j * 64 + 1).astype(f32)
            chosen[part, :] = (place == r).astype(f32).astype(bf16)
            return 0

        lax.fori_loop(0, 12, build, 0)
        high = jnp.floor(its_rank * (1.0 / 256.0))
        which = iota((16, 1536), 0)
        both = jnp.where(which == 0, high, jnp.where(which == 1, its_rank - 256.0 * high, 0.0))
        ranks = dot(both.astype(bf16), chosen[...], NT)
        rank_of = ranks[0:1] * 256.0 + ranks[1:2]
        return iota((1, ROWS), 1) - rank_of.astype(i32), rank_of[:, ROWS - 1 : ROWS].astype(i32)

    everyone = range(GROUPS)

    def repeat(step):
        def once(g, _):
            step(g)
            return 0

        lax.fori_loop(0, GROUPS, once, 0)

    pack(0, 1)
    pl.semaphore_wait(barrier, len(partners))
    first(0, 1)
    second(0, 1, 0)
    pick(0)
    pack(0, 0)
    first(0, 0)
    second(0, 0, 0)
    pick(2)
    pack(0, 2)
    first(0, 2)
    second(0, 2, 0)
    meta_first()

    def other_half(i, _):
        part = pl.ds(pl.multiple_of(i * 64, 64), 64)
        e = embed[part, HALF:WIDTH]
        unit[part, HALF:WIDTH] = (e * jnp.tile(scale[part, :], (1, 4))).astype(bf16)
        return 0

    lax.fori_loop(0, 12, other_half, 0)
    pack(1, 1)
    first(1, 1)
    for d in (1, 3, 2):
        for g in everyone:
            second(0, g, d)
    pack(1, 0)
    first(1, 0)
    second(1, 0, 0)
    pack(1, 2)
    first(1, 2)
    second(1, 1, 0)
    second(1, 2, 0)
    meta_second()
    for d in (0, 1, 3, 2):
        for g in (2, 0, 1):
            third(0, g, d)
    meta_third()
    for d in (1, 3, 2):
        for g in everyone:
            second(1, g, d)
    for g in (2, 0, 1):
        third(1, g, 0)
    for d in (1, 3, 2):
        for g in (2, 0, 1):
            third(1, g, d)
    begin, last_rank = choose()
    repeat(lambda g: unpack(0, g))
    gather()
    unpack(1, 0)
    unpack(1, 1)
    gather_most()
    unpack(1, 2)
    gather_rest()

    landed(from_next.at[0], halo_sem.at[1])
    with_next[...] = dot(own[0], from_next[0], NT)
    landed(from_prev.at[0], halo_sem.at[0])
    with_prev[...] = dot(from_prev[0], own[0], NT)

    here = []
    for j in range(3):
        n = 256 * (j + 1)
        p = slice(256 * j, n)
        s = dot(own[0, 0:n], own[0, p], NT) + dot(own[1, 0:n], own[1, p], NT)
        q, at = iota((n, 256), 0), iota((n, 256), 1) + 256 * j
        s = jnp.where((q >= begin[:, p]) & (q < at), s, -1.0)
        here.append(jnp.max(s, axis=0, keepdims=True))
    best = jnp.concatenate(here, axis=1)

    for h in range(2):
        for g in range(GROUPS):
            for phase in range(2):
                landed(sent0.at[h, g, pl.ds(0, 3)], out_sem.at[h, g, phase])
            landed(unit.at[pl.ds(0, 224)], out_sem.at[h, g, 2])
    landed(meta0.at[pl.ds(0, 3)], mout_sem.at[0])
    landed(meta0.at[pl.ds(0, 3)], mout_sem.at[1])
    landed(flat.at[pl.ds(0, 112)], mout_sem.at[2])

    for i, (lo, hi) in enumerate(PARTS[:2]):
        landed(from_next.at[1, pl.ds(lo, hi - lo)], last_sem.at[i])
        s = with_next[:, lo:hi] + dot(own[1], from_next[1, lo:hi], NT)
        s = jnp.where(iota((ROWS, hi - lo), 0) >= ROWS - 1 - last_rank, s, -1.0)
        answer[:, lo:hi] = jnp.max(s, axis=0, keepdims=True)
    remote(answer, returned, back_out, back_sem, later)

    for i, (lo, hi) in enumerate(PARTS[2:]):
        lo, hi = lo - EDGE, hi - EDGE
        landed(from_prev.at[1, pl.ds(lo, hi - lo)], last_sem.at[2 + i])
        s = with_prev[lo:hi, :] + dot(from_prev[1, lo:hi], own[1], NT)
        s = jnp.where(iota((hi - lo, ROWS), 0) + (lo - REST) >= begin, s, -1.0)
        best = jnp.maximum(best, jnp.max(s, axis=0, keepdims=True))
    landed(from_prev.at[0], halo_out.at[0])
    landed(from_next.at[0], halo_out.at[1])
    for i, (lo, hi) in enumerate(PARTS):
        landed(own.at[1, pl.ds(lo, hi - lo)], last_out.at[i])
    landed(returned, back_sem)
    back = jnp.concatenate([returned[...], jnp.full((1, ROWS - EDGE), -1.0, f32)], axis=1)
    best = jnp.maximum(best, jnp.where(begin < 0, back, -1.0))
    best_ref[...] = best.reshape(ROWS)
    landed(returned, back_out)


def per_device(embed, cluster, rank, target):
    blocks = (2, GROUPS, 4, 4, 4, 2, 16, 128)
    meta = (4, 4, 4, 2, 1, 128)
    dma = pltpu.SemaphoreType.DMA
    best = pl.pallas_call(
        kernel,
        out_shape=pltpu.VMEM((ROWS,), f32),
        in_specs=[
            pl.BlockSpec(memory_space=pl.ANY),
            pl.BlockSpec(memory_space=pl.ANY),
            pl.BlockSpec(memory_space=pl.ANY),
        ],
        out_specs=pl.BlockSpec(memory_space=pltpu.VMEM),
        scratch_shapes=[
            pltpu.VMEM((ROWS,), i32),
            pltpu.VMEM((ROWS,), i32),
            pltpu.VMEM((ROWS, WIDTH), f32),
            pltpu.VMEM((ROWS, 128), f32),
            pltpu.VMEM((GROUPS, DEVICES * DEPTH, ROWS), bf16),
            pltpu.VMEM((ROWS, WIDTH), bf16),
            *[pltpu.VMEM(blocks, bf16)] * 4,
            *[pltpu.VMEM(meta, f32)] * 4,
            pltpu.VMEM((DEVICES, 128), f32),
            pltpu.VMEM((2, GROUPS * 512, HALF), bf16),
            pltpu.VMEM((ROWS, GROUPS * 512), bf16),
            pltpu.VMEM((ROWS, HALF), f32),
            pltpu.VMEM((2, ROWS, HALF), bf16),
            pltpu.VMEM((2, REST, HALF), bf16),
            pltpu.VMEM((2, EDGE, HALF), bf16),
            pltpu.VMEM((REST, ROWS), f32),
            pltpu.VMEM((ROWS, EDGE), f32),
            pltpu.VMEM((1, EDGE), f32),
            pltpu.VMEM((1, EDGE), f32),
            dma((3,)),
            dma((2,)),
            dma((2, GROUPS, 4)),
            dma((2, GROUPS, 4)),
            dma((2, GROUPS)),
            dma((2, GROUPS, 3)),
            dma,
            dma,
            dma,
            dma((3,)),
            dma((2,)),
            dma((2,)),
            dma((4,)),
            dma((4,)),
            dma,
            dma,
        ],
        compiler_params=pltpu.CompilerParams(
            collective_id=0, has_side_effects=True, vmem_limit_bytes=56 * 2**20
        ),
        cost_estimate=pl.CostEstimate(flops=12 * 10**9, bytes_accessed=3 * 2**20, transcendentals=768),
    )(embed, target, rank)
    return best


def solution(mesh):
    in_specs = (P(("grp", "sub"), None), P(("grp", "sub")), P(("grp", "sub")), P(("grp", "sub")))
    out_specs = P(("grp", "sub"))
    return jax.shard_map(
        per_device, mesh=mesh, in_specs=in_specs, out_specs=out_specs, check_vma=False
    )
```

profile of v0, /device:TPU:0, one launch (start us, length us, event | category | flops | bytes accessed | tf_op | source)
XLA Modules:
  0.0 56.8 jit_solution(1441246184671222126)
XLA Ops:
  0.0 56.2 %shard_map.37 = f32[768]{0:T(1024)S(1)} custom-call(f32[768,1024]{1,0:T(8,128)} %embed_hbm.1, s32[768]{0:T(1024)} %target_hbm.1, s32[768]{0:T(1024)} %rank_hbm.1), custom_call_target="tpu_custom_call" | custom-call | flops 12000000000 | bytes 3145728 | tf_op jit(solution)/shard_map/pallas_call | solution.py:412
  56.2 0.6 %copy.5 = f32[768]{0:T(1024)} copy(f32[768]{0:T(1024)S(1)} %shard_map.37) | data formatting | bytes 6144
where the time goes:
time: 56.9 us; the launch traced here: 56.8 us
  Pallas kernels  56.2 us (99%)
  local copies, waits for them, and re-layouts  0.6 us (1%)
    pallas_call x1, Pallas kernels, per_device(): pl.pallas_call(kernel, out_shape=pltpu.VMEM((ROWS,), f32), in_specs=[pl.B...  56.2 us

commit v1 on v0

--- a/solution.py
+++ b/solution.py
@@ -345,11 +345,13 @@
             second(1, g, d)
     for g in (2, 0, 1):
         third(1, g, 0)
-    for d in (1, 3, 2):
+    begin, last_rank = choose()
+    for d in (1, 3):
         for g in (2, 0, 1):
             third(1, g, d)
-    begin, last_rank = choose()
     repeat(lambda g: unpack(0, g))
+    for g in (2, 0, 1):
+        third(1, g, 2)
     gather()
     unpack(1, 0)
     unpack(1, 1)

time: 56.9 us -> 56.5 us (level)
  no operation moved by 1% of the time
where the time goes in v1:
time: 56.5 us; the launch traced here: 56.4 us
  Pallas kernels  55.8 us (99%)
  local copies, waits for them, and re-layouts  0.6 us (1%)
    pallas_call x1, Pallas kernels, per_device(): pl.pallas_call(kernel, out_shape=pltpu.VMEM((ROWS,), f32), in_specs=[pl.B...  55.8 us

profile of v1, /device:TPU:0, one launch (start us, length us, event | category | flops | bytes accessed | tf_op | source)
XLA Modules:
  0.0 56.4 jit_solution(7742909828827295349)
XLA Ops:
  0.0 55.8 %shard_map.37 = f32[768]{0:T(1024)S(1)} custom-call(f32[768,1024]{1,0:T(8,128)} %embed_hbm.1, s32[768]{0:T(1024)} %target_hbm.1, s32[768]{0:T(1024)} %rank_hbm.1), custom_call_target="tpu_custom_call" | custom-call | flops 12000000000 | bytes 3145728 | tf_op jit(solution)/shard_map/pallas_call | solution.py:414
  55.8 0.6 %copy.5 = f32[768]{0:T(1024)} copy(f32[768]{0:T(1024)S(1)} %shard_map.37) | data formatting | bytes 6144

commit v2 on v1

--- a/solution.py
+++ b/solution.py
@@ -18,7 +18,7 @@
 GROUPS = 3
 DEPTH = 4
 DEVICES = 128
-EDGE = 336
+EDGE = 320
 REST = ROWS - EDGE
 PARTS = ((0, 256), (256, EDGE), (EDGE, EDGE + 256), (EDGE + 256, ROWS))
 NT = (((1,), (1,)), ((), ()))
@@ -101,15 +101,19 @@
         picks[g] = (code.astype(i32) == wanted).astype(f32).astype(bf16)
 
     pick(1)
+    for load in loads:
+        load.wait()
+    early = jnp.zeros((DEVICES * DEPTH, HALF), f32)
     for i in range(3):
-        loads[i].wait()
-
+        half = []
         for j in range(8):
             part = slice(i * 256 + j * 32, i * 256 + j * 32 + 32)
             e = embed[part, :]
             squares = jnp.sum(e * e, axis=1, keepdims=True)
             scale[part, :] = jnp.broadcast_to(lax.rsqrt(squares + 1e-06), (32, 128))
-            unit[part, 0:HALF] = (e[:, 0:HALF] * jnp.tile(scale[part, :], (1, 4))).astype(bf16)
+            half.append((e[:, 0:HALF] * lax.rsqrt(squares + 1e-06)).astype(bf16))
+            unit[part, 0:HALF] = half[-1]
+        early += dot(picks[1, :, i * 256 : i * 256 + 256], jnp.concatenate(half, axis=0))
 
     def meta_first():
         lane_slot = iota((DEVICES, ROWS), 0).astype(f32)
@@ -150,7 +154,10 @@
         pltpu.make_async_copy(view(meta2, **here), view(meta3, **here), msem3).start()
 
     def pack(h, g):
-        q = dot(picks[g], unit[:, h * HALF : (h + 1) * HALF]).reshape(64, 8, HALF)
+        finish(h, g, dot(picks[g], unit[:, h * HALF : (h + 1) * HALF]))
+
+    def finish(h, g, q):
+        q = q.reshape(64, 8, HALF)
         r = pltpu.roll(q, 4, 1)
         low = iota((64, 8, 128), 1) < 4
         qs = [q[:, :, 128 * j : 128 * j + 128] for j in range(4)]
@@ -245,7 +252,8 @@
         partly[...] = dot(chosen[:, 0:1024], slots[1, 0:1024])
 
     def gather_rest():
-        for i, (lo, hi) in enumerate(PARTS):
+        for i in (0, 2, 1, 3):
+            lo, hi = PARTS[i]
             rest = dot(chosen[lo:hi, 1024:1536], slots[1, 1024:1536])
             own[1, lo:hi, :] = (partly[lo:hi, :] + rest).astype(bf16)
             if hi <= EDGE:
@@ -302,7 +310,7 @@
 
         lax.fori_loop(0, GROUPS, once, 0)
 
-    pack(0, 1)
+    finish(0, 1, early)
     pl.semaphore_wait(barrier, len(partners))
     first(0, 1)
     second(0, 1, 0)

time: 56.5 us -> 56.1 us (level)
  no operation moved by 1% of the time
where the time goes in v2:
time: 56.1 us; the launch traced here: 56 us
  Pallas kernels  55.4 us (99%)
  local copies, waits for them, and re-layouts  0.6 us (1%)
    pallas_call x1, Pallas kernels, per_device(): pl.pallas_call(kernel, out_shape=pltpu.VMEM((ROWS,), f32), in_specs=[pl.B...  55.4 us

profile of v2, /device:TPU:0, one launch (start us, length us, event | category | flops | bytes accessed | tf_op | source)
XLA Modules:
  0.0 56.0 jit_solution(11031848184180772087)
XLA Ops:
  0.0 55.4 %shard_map.37 = f32[768]{0:T(1024)S(1)} custom-call(f32[768,1024]{1,0:T(8,128)} %embed_hbm.1, s32[768]{0:T(1024)} %target_hbm.1, s32[768]{0:T(1024)} %rank_hbm.1), custom_call_target="tpu_custom_call" | custom-call | flops 12000000000 | bytes 3145728 | tf_op jit(solution)/shard_map/pallas_call | solution.py:422
  55.4 0.6 %copy.5 = f32[768]{0:T(1024)} copy(f32[768]{0:T(1024)S(1)} %shard_map.37) | data formatting | bytes 6144

commit v3 on v2

--- a/solution.py
+++ b/solution.py
@@ -367,11 +367,6 @@
     unpack(1, 2)
     gather_rest()
 
-    landed(from_next.at[0], halo_sem.at[1])
-    with_next[...] = dot(own[0], from_next[0], NT)
-    landed(from_prev.at[0], halo_sem.at[0])
-    with_prev[...] = dot(from_prev[0], own[0], NT)
-
     here = []
     for j in range(3):
         n = 256 * (j + 1)
@@ -381,6 +376,11 @@
         s = jnp.where((q >= begin[:, p]) & (q < at), s, -1.0)
         here.append(jnp.max(s, axis=0, keepdims=True))
     best = jnp.concatenate(here, axis=1)
+
+    landed(from_next.at[0], halo_sem.at[1])
+    with_next[...] = dot(own[0], from_next[0], NT)
+    landed(from_prev.at[0], halo_sem.at[0])
+    with_prev[...] = dot(from_prev[0], own[0], NT)
 
     for h in range(2):
         for g in range(GROUPS):

time: 56.1 us -> 56.5 us (level)
  no operation moved by 1% of the time
where the time goes in v3:
time: 56.5 us; the launch traced here: 56.4 us
  Pallas kernels  55.8 us (99%)
  local copies, waits for them, and re-layouts  0.6 us (1%)
    pallas_call x1, Pallas kernels, per_device(): pl.pallas_call(kernel, out_shape=pltpu.VMEM((ROWS,), f32), in_specs=[pl.B...  55.8 us

profile of v3, /device:TPU:0, one launch (start us, length us, event | category | flops | bytes accessed | tf_op | source)
XLA Modules:
  0.0 56.4 jit_solution(4629601881605433787)
XLA Ops:
  0.0 55.8 %shard_map.37 = f32[768]{0:T(1024)S(1)} custom-call(f32[768,1024]{1,0:T(8,128)} %embed_hbm.1, s32[768]{0:T(1024)} %target_hbm.1, s32[768]{0:T(1024)} %rank_hbm.1), custom_call_target="tpu_custom_call" | custom-call | flops 12000000000 | bytes 3145728 | tf_op jit(solution)/shard_map/pallas_call | solution.py:422
  55.8 0.6 %copy.5 = f32[768]{0:T(1024)} copy(f32[768]{0:T(1024)S(1)} %shard_map.37) | data formatting | bytes 6144
